TPU v7x, 512 devices: a whole 4x4x16 slice. The times are simulated.
512 devices in a mesh: clip: 32 (over z, core), frame: 16 (over x, y).
Axes of the slice: x: 4, y: 4, z: 16, core: 2. Of those that a mesh axis runs over, the one named last changes fastest.
Arguments:
- inputs: bfloat16 [32, 5, 128, 64, 128], P('clip', None, 'frame'), may hold values from -16 to 16
- norm_gain: float32 [128], replicated, may hold values from 0.1 to 1.9
- norm_bias: float32 [128], replicated, may hold values from -3 to 3
- conv_weight: bfloat16 [3, 3, 3, 128, 128], replicated, may hold values from -0.109375 to 0.109375
- conv_bias: float32 [128], replicated, may hold values from -3 to 3
- down_weight: bfloat16 [3, 3, 128, 128], replicated, may hold values from -0.1875 to 0.1875
- down_bias: float32 [128], replicated, may hold values from -3 to 3
- time_weight: bfloat16 [3, 128, 128], replicated, may hold values from -0.3125 to 0.3125
- time_bias: float32 [128], replicated, may hold values from -3 to 3
- head_weight: bfloat16 [128, 32], replicated, may hold values from -0.5 to 0.5
- head_bias: float32 [32], replicated, may hold values from -3 to 3
- tile_shard: int32 [32, 3, 512], P('clip', None, 'frame'), may hold values from 0 to 31, as said below
- tile_slot: int32 [32, 3, 512], P('clip', None, 'frame'), may hold values from 0 to 1023, as said below
Outputs:
- packed: bfloat16 [3, 32768, 128], P(None, ('clip', 'frame'))
Inputs may be any that keep to these rules, and one draw needn't show every extreme that they name: `tile_shard`: tiles t of one clip and reduced frame with t // 32 = g form block g. In every such block at most 2 tiles go to one shard, and in every reduced frame and block some shard receives exactly 2 tiles from every clip. `tile_slot`: the tiles of block g sent to one shard in one reduced frame have distinct slots from g * 64 to (g + 1) * 64 - 1.
All inputs are finite; a program needn't handle non-finite values.
Results may differ from a plain program's by a relative error of at most 0.006.
Values may be sent and summed in bfloat16 or wider, within the bound.
No kernel may reach another device: no remote copies, remote signals or barrier semaphores. Data moves between devices by JAX's collectives and lax.ppermute only.
A program may use at most 64 MiB of HBM per device.

v0:
```python
import jax
import jax.numpy as jnp
from jax import lax
from jax.sharding import PartitionSpec as P

GROUPS = 32
EPSILON = 1e-06


def with_halo(cells, sides, width):
    for axis, dim in sides:
        count = lax.axis_size(axis)
        ends = count - 1
        head = lax.slice_in_dim(cells, 0, width, axis=dim)
        tail = lax.slice_in_dim(cells, cells.shape[dim] - width, cells.shape[dim], axis=dim)
        cells = jnp.concatenate(
            [
                lax.ppermute(tail, axis, [(i, (i + 1) % count) for i in range(ends)]),
                cells,
                lax.ppermute(head, axis, [((i + 1) % count, i) for i in range(ends)]),
            ],
            axis=dim,
        )
    return cells


def from_behind(block, axis, distance):
    devices = range(lax.axis_size(axis))
    route = [(i - distance, i) for i in devices if i - distance in devices]
    return lax.ppermute(block, axis, route)


def causal_mix(stacked_pad, weight, bias_vec, frame_count, row_count, col_count):
    channels = weight.shape[-1]
    col_stack = jnp.concatenate(
        [stacked_pad[:, :, col_tap : col_tap + col_count] for col_tap in range(3)], axis=-1
    )
    accum_sum = jnp.zeros((frame_count * row_count * col_count, channels), jnp.float32)
    for time_tap in range(3):
        for row_tap in range(3):
            stacked = col_stack[time_tap : time_tap + frame_count, row_tap : row_tap + row_count]
            accum_sum = accum_sum + jnp.dot(
                stacked.reshape(-1, 3 * channels),
                weight[time_tap, row_tap].reshape(3 * channels, channels),
                preferred_element_type=jnp.float32,
            )
    return accum_sum.reshape(frame_count, row_count, col_count, channels) + bias_vec


def strided_mix(padded, weight, bias_vec, row_out, col_out):
    frame_count = padded.shape[0]
    channels = weight.shape[-1]
    accum_sum = jnp.zeros((frame_count * row_out * col_out, channels), jnp.float32)
    for row_tap in range(3):
        window = padded[:, row_tap : row_tap + 2 * row_out : 2]
        stacked = jnp.concatenate(
            [window[:, :, col_tap : col_tap + 2 * col_out : 2] for col_tap in range(3)], axis=-1
        )
        accum_sum = accum_sum + jnp.dot(
            stacked.reshape(-1, 3 * channels),
            weight[row_tap].reshape(3 * channels, channels),
            preferred_element_type=jnp.float32,
        )
    return accum_sum.reshape(frame_count, row_out, col_out, channels) + bias_vec


def time_mix(padded, weight, bias_vec, lat_count):
    channels = weight.shape[-1]
    rest = padded.shape[1:3]
    accum_sum = jnp.zeros((lat_count * rest[0] * rest[1], channels), jnp.float32)
    for time_tap in range(3):
        window = padded[time_tap : time_tap + 2 * lat_count - 1 : 2]
        accum_sum = accum_sum + jnp.dot(
            window.reshape(-1, channels), weight[time_tap], preferred_element_type=jnp.float32
        )
    return accum_sum.reshape(lat_count, rest[0], rest[1], channels) + bias_vec


def project_head(lat_mixed, head_weight, head_bias):
    lat_count, row_count, col_count, channels = lat_mixed.shape
    out_channels = head_weight.shape[1]
    latent = (
        jnp.dot(lat_mixed.reshape(-1, channels), head_weight, preferred_element_type=jnp.float32)
        + head_bias
    )
    return latent.astype(jnp.bfloat16).reshape(lat_count, row_count, col_count, out_channels)


def to_tiles(latent):
    lat_count, row_count, col_count, out_channels = latent.shape
    split_up = latent.reshape(lat_count, row_count // 2, 2, col_count // 2, 2, out_channels)
    split_up = split_up.transpose(0, 1, 3, 2, 4, 5)
    return split_up.reshape(lat_count, row_count // 2 * (col_count // 2), 4 * out_channels)


def normalize(block, group_mean, inverse, norm_gain, norm_bias):
    shape_in = block.shape
    grouped = block.astype(jnp.float32).reshape(shape_in[:-1] + (GROUPS, shape_in[-1] // GROUPS))
    normed = ((grouped - group_mean[:, None]) * inverse[:, None]).reshape(shape_in)
    return jax.nn.silu(normed * norm_gain + norm_bias)


def local(
    inputs,
    norm_gain,
    norm_bias,
    conv_weight,
    conv_bias,
    down_weight,
    down_bias,
    time_weight,
    time_bias,
    head_weight,
    head_bias,
    tile_shard,
    tile_slot,
):
    activations = inputs[0]
    frame_count, row_count, col_count, channels = activations.shape
    frame_devs = lax.axis_size("frame")
    position = lax.axis_index("frame")
    entries = frame_count * frame_devs * row_count * col_count * (channels // GROUPS)
    grouped = activations.reshape(frame_count, row_count, col_count, GROUPS, channels // GROUPS)
    local_sum = jnp.sum(grouped, axis=(0, 1, 2, 4), dtype=jnp.float32)
    group_mean = lax.psum(local_sum, "frame") / entries
    centred = grouped.astype(jnp.float32) - group_mean[:, None]
    group_var = lax.psum(jnp.sum(centred * centred, axis=(0, 1, 2, 4)), "frame") / entries
    inverse = lax.rsqrt(group_var + EPSILON)
    hidden = normalize(activations, group_mean, inverse, norm_gain, norm_bias).astype(jnp.bfloat16)
    hidden_ext = with_halo(hidden, (("frame", 1),), 1)
    hidden_pad = jnp.pad(hidden_ext, ((2, 0), (0, 0), (1, 1), (0, 0)))
    mixed = causal_mix(hidden_pad, conv_weight, conv_bias, frame_count, row_count, col_count)
    with_skip = (activations.astype(jnp.float32) + mixed).astype(jnp.bfloat16)
    following = from_behind(with_skip[:, :1], "frame", -1)
    padded = jnp.pad(
        jnp.concatenate([with_skip, following], axis=1), ((0, 0), (0, 0), (0, 1), (0, 0))
    )
    reduced = strided_mix(padded, down_weight, down_bias, row_count // 2, col_count // 2).astype(
        jnp.bfloat16
    )
    time_pad = jnp.pad(reduced, ((2, 0), (0, 0), (0, 0), (0, 0)))
    lat_mixed = time_mix(time_pad, time_weight, time_bias, (frame_count + 1) // 2).astype(
        jnp.bfloat16
    )
    latent = project_head(lat_mixed, head_weight, head_bias)
    patch_tiles = to_tiles(latent)
    lat_count = patch_tiles.shape[0]
    tile_count = patch_tiles.shape[1]
    tile_width = patch_tiles.shape[2]
    shard_ids = tile_shard[0]
    shards = lax.axis_size("clip")
    pair_slots = 2 * (tile_count // shards)
    slot_block = shards * pair_slots
    slot_ids = tile_slot[0] - position * slot_block
    matches = (shard_ids[:, :, None] == jnp.arange(shards, dtype=jnp.int32)[None, None, :]).astype(
        jnp.int32
    )
    rank_in = jnp.sum((jnp.cumsum(matches, axis=1) - 1) * matches, axis=-1)
    target = shard_ids * pair_slots + rank_in
    chooser = target[:, None, :] == jnp.arange(slot_block, dtype=jnp.int32)[None, :, None]
    outgoing = jnp.einsum(
        "lpt,ltc->lpc",
        chooser.astype(jnp.bfloat16),
        patch_tiles,
        preferred_element_type=jnp.float32,
    ).astype(jnp.bfloat16)
    filled = jnp.any(chooser, axis=-1).astype(jnp.int32)
    out_slot = jnp.sum(jnp.where(chooser, slot_ids[:, None, :], 0), axis=-1) + slot_block * (
        1 - filled
    )
    outgoing = outgoing.reshape(lat_count, shards, pair_slots, tile_width)
    out_slot = out_slot.reshape(lat_count, shards, pair_slots)
    arrived, arrived_slot = (
        lax.all_to_all(outgoing, "clip", split_axis=1, concat_axis=1, tiled=True),
        lax.all_to_all(out_slot, "clip", split_axis=1, concat_axis=1, tiled=True),
    )
    arrived = arrived.reshape(lat_count, slot_block, tile_width)
    arrived_slot = arrived_slot.reshape(lat_count, slot_block)
    placer = (
        arrived_slot[:, None, :] == jnp.arange(slot_block, dtype=jnp.int32)[None, :, None]
    ).astype(jnp.bfloat16)
    packed = jnp.einsum("lqp,lpc->lqc", placer, arrived, preferred_element_type=jnp.float32)
    return packed.astype(jnp.bfloat16)


def solution(mesh):
    placed = (
        P("clip", None, "frame", None, None),
        P(),
        P(),
        P(),
        P(),
        P(),
        P(),
        P(),
        P(),
        P(),
        P(),
        P("clip", None, "frame"),
        P("clip", None, "frame"),
    )
    return jax.shard_map(
        local,
        mesh=mesh,
        in_specs=placed,
        out_specs=P(None, ("clip", "frame"), None),
        check_vma=False,
    )
```

profile of v0, /device:TPU:8, one launch (start us, length us, event | category | flops | bytes accessed | tf_op | source)
XLA Modules:
  0.0 159.9 jit_solution(9977026523880705705)
XLA Ops:
  0.0 1.5 convert_reduce_fusion
  1.5 0.1 reduce_sum.53
  1.6 0.1 reduce_sum.54
  1.7 41.3 %psum.14 = f32[32]{0:T(128)S(1)} all-reduce(f32[32]{0:T(128)S(1)} %reduce_sum.54), channel_id=1, replica_groups=mesh['clip'=32,'frame'=16] {'frame'}, use_global_device_ids=true, to_apply=%region_6.7 | all-reduce | flops 32 | bytes 256 | tf_op jit(solution)/shard_map/psum | solution.py:125
  43.0 0.1 sub.53
  43.1 0.1 sub.54
  43.2 1.5 fusion.20
  44.7 0.1 reduce_sum.56
  44.8 0.1 reduce_sum.57
  45.0 35.5 %psum.15 = f32[32]{0:T(128)S(1)} all-reduce(f32[32]{0:T(128)S(1)} %reduce_sum.57), channel_id=1, replica_groups=mesh['clip'=32,'frame'=16] {'frame'}, use_global_device_ids=true, to_apply=%region_9.10 | all-reduce | flops 32 | bytes 256 | tf_op jit(solution)/shard_map/psum | solution.py:127
  80.4 0.1 mul.60
  80.5 0.1 mul.61
  80.6 0.5 fusion.17
  81.2 1.9 %collective-permute-start = (bf16[5,1,64,128]{3,2,1,0:T(8,128)(2,1)S(1)}, bf16[5,1,64,128]{3,2,1,0:T(8,128)(2,1)S(1)}, u32[]{:S(2)}, u32[]{:S(2)}) collective-permute-start(bf16[5,1,64,128]{3,2,1,0:T(8,128)(2,1)S(1)} %get-tuple-element.29), channel_id=1, source_target_pairs={{0,1},{1,2},{2,3},{3,4},{4,5},{5,6},{6,7},{7,8},{8,9},{9,10},{10,1... | collective-permute-start | bytes 245768 | tf_op jit(solution)/shard_map/ppermute | solution.py:18
  83.1 3.9 %collective-permute-start.1 = (bf16[5,1,64,128]{3,2,1,0:T(8,128)(2,1)S(1)}, bf16[5,1,64,128]{3,2,1,0:T(8,128)(2,1)S(1)}, u32[]{:S(2)}, u32[]{:S(2)}) collective-permute-start(bf16[5,1,64,128]{3,2,1,0:T(8,128)(2,1)S(1)} %get-tuple-element.30), channel_id=1, source_target_pairs={{1,0},{2,1},{3,2},{4,3},{5,4},{6,5},{7,6},{8,7},{9,8},{10,9},{11,1... | collective-permute-start | bytes 245768 | tf_op jit(solution)/shard_map/ppermute | solution.py:20
  87.0 0.1 fusion.35
  87.2 0.2 select_reduce_fusion.1
  87.4 0.1 fusion.34
  87.5 0.1 select_reduce_fusion
  87.7 0.7 copy.24
  88.4 15.3 %all-to-all-start = ((s32[3,32,2]{0,2,1:T(2,128)}), s32[3,32,2]{0,2,1:T(2,128)S(1)}, u32[]{:S(2)}, u32[]{:S(2)}) async-start(s32[3,32,2]{0,2,1:T(2,128)} %bitcast), calls=%async_computation | async-start | bytes 65536 | tf_op jit(solution)/shard_map/all_to_all | solution.py:175
  103.8 0.4 fusion.23
  104.2 0.8 fusion.47
  105.0 0.6 pad_maximum_fusion
  105.6 7.0 %fusion.46 = (bf16[5,8,64,384]{3,2,1,0:T(8,128)(2,1)S(1)}, bf16[5,8,64,384]{3,2,1,0:T(8,128)(2,1)S(1)}, bf16[5,8,64,384]{3,2,1,0:T(8,128)(2,1)S(1)}, bf16[5,8,64...) fusion(bf16[7,10,64,384]{3,2,1,0:T(8,128)(2,1)S(1)} %pad_maximu, ...), kind=kLoop, calls=%fused_computation.85 | loop fusion | bytes 35389440 | tf_op jit(solution)/shard_map/slice | solution.py:41
  112.6 2.4 %fusion.52 = f32[2560,128]{1,0:T(8,128)S(1)} fusion(bf16[2560,384]{1,0:T(8,128)(2,1)} %bitcast.120, bf16[384,128]{1,0:T(8,128)(2,1)S(1)} %bitcast.126), kind=kOutput, calls=%fused_computation.91 | convolution fusion | flops 251658240 | bytes 3375104 | tf_op jit(solution)/shard_map/dot_general | solution.py:42
  115.0 0.7 convolution_add_fusion.7
  115.7 0.7 convolution_add_fusion.6
  116.4 0.7 convolution_add_fusion.5
  117.1 0.7 convolution_add_fusion.4
  117.8 0.7 convolution_add_fusion.3
  118.5 0.7 convolution_add_fusion.2
  119.2 0.7 convolution_add_fusion.1
  119.9 0.7 convolution_add_fusion
  120.6 0.2 fusion.18
  120.8 2.1 %collective-permute-start.2 = (bf16[5,1,64,128]{3,2,1,0:T(8,128)(2,1)S(1)}, bf16[5,1,64,128]{3,2,1,0:T(8,128)(2,1)S(1)}, u32[]{:S(2)}, u32[]{:S(2)}) collective-permute-start(bf16[5,1,64,128]{3,2,1,0:T(8,128)(2,1)S(1)} %slice.194), channel_id=1, source_target_pairs={{1,0},{2,1},{3,2},{4,3},{5,4},{6,5},{7,6},{8,7},{9,8},{10,9},{11,1... | collective-permute-start | bytes 245768 | tf_op jit(solution)/shard_map/ppermute | solution.py:30
  123.0 4.4 %collective-permute-done.2 = bf16[5,1,64,128]{3,2,1,0:T(8,128)(2,1)S(1)} collective-permute-done((bf16[5,1,64,128]{3,2,1,0:T(8,128)(2,1)S(1)}, bf16[5,1,64,128]{3,2,1,0:T(8,128)(2,1)S(1)}, u32[]{:S(2)}, u32[]{:S(2)}) %collective-permute-start.2) | collective-permute-done | bytes 81952 | tf_op jit(solution)/shard_map/ppermute | solution.py:30
  127.4 0.1 fusion.49
  127.5 0.2 slice.170
  127.8 0.2 slice.171
  128.0 0.2 slice.172
  128.2 0.2 slice.165
  128.5 0.2 slice.166
  128.7 0.2 slice.167
  128.9 0.2 slice.160
  129.1 0.2 slice.161
  129.4 0.2 slice.162
  129.6 0.1 pad_maximum_fusion.1
  129.7 0.3 fusion.53
  130.0 0.1 pad_maximum_fusion.3
  130.1 0.1 pad_maximum_fusion.2
  130.2 0.3 convolution_add_fusion.9
  130.5 0.3 convolution_add_fusion.8
  130.9 0.5 copy-done.5
  131.4 0.2 fusion.39
  131.5 0.2 convolution_add_fusion.11
  131.7 0.3 fusion.30
  132.0 0.1 copy.20
  132.2 0.1 reshape.124
  132.4 0.3 convolution_convert_fusion.1
  132.7 0.7 copy.22
  133.3 12.0 %all-to-all-start.1 = ((bf16[3,32,2,128]{3,2,0,1:T(2,128)(2,1)}), bf16[3,32,2,128]{3,2,0,1:T(2,128)(2,1)S(1)}, u32[]{:S(2)}, u32[]{:S(2)}) async-start(bf16[3,32,2,128]{3,2,0,1:T(2,128)(2,1)} %copy.22), calls=%async_computation.1 | async-start | bytes 98304 | tf_op jit(solution)/shard_map/all_to_all | solution.py:174
  145.4 13.6 %all-to-all-done.1 = bf16[3,32,2,128]{3,2,0,1:T(2,128)(2,1)S(1)} async-done(((bf16[3,32,2,128]{3,2,0,1:T(2,128)(2,1)}), bf16[3,32,2,128]{3,2,0,1:T(2,128)(2,1)S(1)}, u32[]{:S(2)}, u32[]{:S(2)}) %all-to-all-start.1) | async-done | bytes 49184 | tf_op jit(solution)/shard_map/all_to_all | solution.py:174
  159.1 0.8 convolution_convert_fusion
  (48 shorter events, 0.6 us)
Async XLA Ops:
  0.0 131.7 %copy-start = (bf16[128,32]{0,1:T(8,128)(2,1)S(1)}, bf16[128,32]{0,1:T(8,128)(2,1)}, u32[]{:S(2)}) copy-start(bf16[128,32]{0,1:T(8,128)(2,1)} %param.22) | copy-start | bytes 24580
  0.0 80.6 %copy-start.1 = (bf16[1,5,8,64,128]{4,3,2,1,0:T(8,128)(2,1)S(1)}, bf16[1,5,8,64,128]{4,3,2,1,0:T(8,128)(2,1)}, u32[]{:S(2)}) copy-start(bf16[1,5,8,64,128]{4,3,2,1,0:T(8,128)(2,1)} %param.13) | copy-start | bytes 1966084
  0.0 80.6 %copy-start.9 = (f32[128]{0:T(128)S(1)}, f32[128]{0:T(128)}, u32[]{:S(2)}) copy-start(f32[128]{0:T(128)} %param.14) | copy-start | bytes 1540
  0.0 80.6 %copy-start.8 = (f32[128]{0:T(128)S(1)}, f32[128]{0:T(128)}, u32[]{:S(2)}) copy-start(f32[128]{0:T(128)} %param.15) | copy-start | bytes 1540
  1.5 85.5 %copy-start.6 = (s32[1,3,32]{2,0,1:T(1,128)S(1)}, s32[1,3,32]{2,0,1:T(1,128)}, u32[]{:S(2)}) copy-start(s32[1,3,32]{2,0,1:T(1,128)} %param.24) | copy-start | bytes 1156
  43.0 44.4 %copy-start.7 = (s32[1,3,32]{2,0,1:T(1,128)S(1)}, s32[1,3,32]{2,0,1:T(1,128)}, u32[]{:S(2)}) copy-start(s32[1,3,32]{2,0,1:T(1,128)} %param.25) | copy-start | bytes 1156
  43.2 60.5 %copy-start.3 = (bf16[3,3,3,128,128]{4,3,2,1,0:T(8,128)(2,1)S(1)}, bf16[3,3,3,128,128]{4,3,2,1,0:T(8,128)(2,1)}, u32[]{:S(2)}) copy-start(bf16[3,3,3,128,128]{4,3,2,1,0:T(8,128)(2,1)} %param.16) | copy-start | bytes 2654212
  81.2 22.6 %collective-permute-start = (bf16[5,1,64,128]{3,2,1,0:T(8,128)(2,1)S(1)}, bf16[5,1,64,128]{3,2,1,0:T(8,128)(2,1)S(1)}, u32[]{:S(2)}, u32[]{:S(2)}) collective-permute-start(bf16[5,1,64,128]{3,2,1,0:T(8,128)(2,1)S(1)} %get-tuple-element.29), channel_id=1, source_target_pairs={{0,1},{1,2},{2,3},{3,4},{4,5},{5,6},{6,7},{7,8},{8,9},{9,10},{10,1... | collective-permute-start | bytes 245768 | tf_op jit(solution)/shard_map/ppermute | solution.py:18
  83.1 20.7 %collective-permute-start.1 = (bf16[5,1,64,128]{3,2,1,0:T(8,128)(2,1)S(1)}, bf16[5,1,64,128]{3,2,1,0:T(8,128)(2,1)S(1)}, u32[]{:S(2)}, u32[]{:S(2)}) collective-permute-start(bf16[5,1,64,128]{3,2,1,0:T(8,128)(2,1)S(1)} %get-tuple-element.30), channel_id=1, source_target_pairs={{1,0},{2,1},{3,2},{4,3},{5,4},{6,5},{7,6},{8,7},{9,8},{10,9},{11,1... | collective-permute-start | bytes 245768 | tf_op jit(solution)/shard_map/ppermute | solution.py:20
  88.4 45.0 %all-to-all-start = ((s32[3,32,2]{0,2,1:T(2,128)}), s32[3,32,2]{0,2,1:T(2,128)S(1)}, u32[]{:S(2)}, u32[]{:S(2)}) async-start(s32[3,32,2]{0,2,1:T(2,128)} %bitcast), calls=%async_computation | async-start | bytes 65536 | tf_op jit(solution)/shard_map/all_to_all | solution.py:175
  112.6 2.4 %copy-start.2 = (bf16[5,8,64,384]{3,2,1,0:T(8,128)(2,1)S(1)}, bf16[5,8,64,384]{3,2,1,0:T(8,128)(2,1)}, u32[]{:S(2)}) copy-start(bf16[5,8,64,384]{3,2,1,0:T(8,128)(2,1)} %get-tuple-element.12) | copy-start | bytes 5898244
  119.9 0.7 copy-start.13
  120.6 2.4 %copy-start.4 = (bf16[3,3,128,128]{3,2,1,0:T(8,128)(2,1)S(1)}, bf16[3,3,128,128]{3,2,1,0:T(8,128)(2,1)}, u32[]{:S(2)}) copy-start(bf16[3,3,128,128]{3,2,1,0:T(8,128)(2,1)} %param.18) | copy-start | bytes 884740
  120.8 6.5 %collective-permute-start.2 = (bf16[5,1,64,128]{3,2,1,0:T(8,128)(2,1)S(1)}, bf16[5,1,64,128]{3,2,1,0:T(8,128)(2,1)S(1)}, u32[]{:S(2)}, u32[]{:S(2)}) collective-permute-start(bf16[5,1,64,128]{3,2,1,0:T(8,128)(2,1)S(1)} %slice.194), channel_id=1, source_target_pairs={{1,0},{2,1},{3,2},{4,3},{5,4},{6,5},{7,6},{8,7},{9,8},{10,9},{11,1... | collective-permute-start | bytes 245768 | tf_op jit(solution)/shard_map/ppermute | solution.py:30
  130.2 0.7 copy-start.10
  130.5 0.9 copy-start.5
  130.5 1.2 copy-start.11
  130.5 1.2 copy-start.12
  133.3 25.8 %all-to-all-start.1 = ((bf16[3,32,2,128]{3,2,0,1:T(2,128)(2,1)}), bf16[3,32,2,128]{3,2,0,1:T(2,128)(2,1)S(1)}, u32[]{:S(2)}, u32[]{:S(2)}) async-start(bf16[3,32,2,128]{3,2,0,1:T(2,128)(2,1)} %copy.22), calls=%async_computation.1 | async-start | bytes 98304 | tf_op jit(solution)/shard_map/all_to_all | solution.py:174
where the time goes:
time: 160 us
  blocking collectives  76.7 us (48%)
  starting transfers between devices  35.3 us (22%)
  waiting for transfers between devices  18 us (11%)
  local copies, waits for them, and re-layouts  12.9 us (8%)
  matrix products  10.4 us (6%)
  other arithmetic  5.89 us (4%)
    psum x1, blocking collectives, local(): group_mean = lax.psum(local_sum, 'frame') / entries  41.3 us
    psum x1, blocking collectives, local(): lax.psum(jnp.sum(centred * centred, axis=(0, 1, 2, 4)), 'frame') / entries  35.5 us
    all_to_all x1, starting transfers between devices, local(): lax.all_to_all(out_slot, 'clip', split_axis=1, concat_axis=1, tiled=True)  15.3 us
    all_to_all x1, waiting for transfers between devices, local(): lax.all_to_all(outgoing, 'clip', split_axis=1, concat_axis=1, tiled=True)  13.6 us
    all_to_all x1, starting transfers between devices, local(): lax.all_to_all(outgoing, 'clip', split_axis=1, concat_axis=1, tiled=True)  12 us
    dot_general x9, matrix products, causal_mix(): jnp.dot(stacked.reshape(-1, 3 * channels), weight[time_tap, row_tap].resh...  7.85 us
    slice x1, local copies, waits for them, and re-layouts, causal_mix(): col_stack[time_tap:time_tap + frame_count, row_tap:row_tap + row_count]  7.03 us
    ppermute x1, waiting for transfers between devices, from_behind(): return lax.ppermute(block, axis, route)  4.37 us
  transfers between devices with their start and end apart: 5, of which 2 were waited for; matrix products, arithmetic and copies ran while one was open for 15% of the time, Pallas kernels for 0%

commit v1 on v0

--- a/solution.py
+++ b/solution.py
@@ -171,7 +171,12 @@
     outgoing = outgoing.reshape(lat_count, shards, pair_slots, tile_width)
     out_slot = out_slot.reshape(lat_count, shards, pair_slots)
     arrived, arrived_slot = (
-        lax.all_to_all(outgoing, "clip", split_axis=1, concat_axis=1, tiled=True),
+        jnp.concatenate(
+            lax.all_to_all(
+                jnp.stack(jnp.split(outgoing, lax.axis_size("clip"), axis=1)), "clip", 0, 0
+            ),
+            axis=1,
+        ),
         lax.all_to_all(out_slot, "clip", split_axis=1, concat_axis=1, tiled=True),
     )
     arrived = arrived.reshape(lat_count, slot_block, tile_width)

time: 160 us -> 178 us (1.11)
  local copies, waits for them, and re-layouts: 12.9 us -> 30.4 us
    unnamed x30 -> x61, local copies, waits for them, and re-layouts: 0.55 us -> 18.1 us
  transfers between devices with their start and end apart: 5 -> 5, of which waited for: 2 -> 2; matrix products, arithmetic and copies ran while one was open for 15% -> 23% of each run, Pallas kernels for 0% -> 0%
where the time goes in v1:
time: 178 us; the launch traced here: 177 us
  blocking collectives  76.7 us (43%)
  starting transfers between devices  35.3 us (20%)
  local copies, waits for them, and re-layouts  30.4 us (17%)
  waiting for transfers between devices  18 us (10%)
  matrix products  10.4 us (6%)
  other arithmetic  5.89 us (3%)
    psum x1, blocking collectives, local(): group_mean = lax.psum(local_sum, 'frame') / entries  41.3 us
    psum x1, blocking collectives, local(): lax.psum(jnp.sum(centred * centred, axis=(0, 1, 2, 4)), 'frame') / entries  35.5 us
    unnamed x61, local copies, waits for them, and re-layouts  18.1 us
    all_to_all x1, starting transfers between devices, local(): lax.all_to_all(out_slot, 'clip', split_axis=1, concat_axis=1, tiled=True)  15.3 us
    all_to_all x1, waiting for transfers between devices, local(): lax.all_to_all(jnp.stack(jnp.split(outgoing, lax.axis_size('clip'), axis=...  13.6 us
    all_to_all x1, starting transfers between devices, local(): lax.all_to_all(jnp.stack(jnp.split(outgoing, lax.axis_size('clip'), axis=...  12 us
    dot_general x9, matrix products, causal_mix(): jnp.dot(stacked.reshape(-1, 3 * channels), weight[time_tap, row_tap].resh...  7.85 us
    slice x1, local copies, waits for them, and re-layouts, causal_mix(): col_stack[time_tap:time_tap + frame_count, row_tap:row_tap + row_count]  7.03 us
  transfers between devices with their start and end apart: 5, of which 2 were waited for; matrix products, arithmetic and copies ran while one was open for 23% of the time, Pallas kernels for 0%

profile of v1, /device:TPU:8, one launch (start us, length us, event | category | flops | bytes accessed | tf_op | source)
XLA Modules:
  0.0 177.3 jit_solution(1839432143904861738)
XLA Ops:
  0.0 1.5 convert_reduce_fusion
  1.7 41.3 %psum.14 = f32[32]{0:T(128)S(1)} all-reduce(f32[32]{0:T(128)S(1)} %reduce_sum.54), channel_id=1, replica_groups=mesh['clip'=32,'frame'=16] {'frame'}, use_global_device_ids=true, to_apply=%region_6.7 | all-reduce | flops 32 | bytes 256 | tf_op jit(solution)/shard_map/psum | solution.py:125
  43.2 1.5 fusion.20
  45.0 35.5 %psum.15 = f32[32]{0:T(128)S(1)} all-reduce(f32[32]{0:T(128)S(1)} %reduce_sum.57), channel_id=1, replica_groups=mesh['clip'=32,'frame'=16] {'frame'}, use_global_device_ids=true, to_apply=%region_9.10 | all-reduce | flops 32 | bytes 256 | tf_op jit(solution)/shard_map/psum | solution.py:127
  80.6 0.5 fusion.17
  81.2 1.9 %collective-permute-start = (bf16[5,1,64,128]{3,2,1,0:T(8,128)(2,1)S(1)}, bf16[5,1,64,128]{3,2,1,0:T(8,128)(2,1)S(1)}, u32[]{:S(2)}, u32[]{:S(2)}) collective-permute-start(bf16[5,1,64,128]{3,2,1,0:T(8,128)(2,1)S(1)} %get-tuple-element.29), channel_id=1, source_target_pairs={{0,1},{1,2},{2,3},{3,4},{4,5},{5,6},{6,7},{7,8},{8,9},{9,10},{10,1... | collective-permute-start | bytes 245768 | tf_op jit(solution)/shard_map/ppermute | solution.py:18
  83.1 3.9 %collective-permute-start.1 = (bf16[5,1,64,128]{3,2,1,0:T(8,128)(2,1)S(1)}, bf16[5,1,64,128]{3,2,1,0:T(8,128)(2,1)S(1)}, u32[]{:S(2)}, u32[]{:S(2)}) collective-permute-start(bf16[5,1,64,128]{3,2,1,0:T(8,128)(2,1)S(1)} %get-tuple-element.30), channel_id=1, source_target_pairs={{1,0},{2,1},{3,2},{4,3},{5,4},{6,5},{7,6},{8,7},{9,8},{10,9},{11,1... | collective-permute-start | bytes 245768 | tf_op jit(solution)/shard_map/ppermute | solution.py:20
  87.7 0.7 copy.150
  88.4 15.3 %all-to-all-start = ((s32[3,32,2]{0,2,1:T(2,128)}), s32[3,32,2]{0,2,1:T(2,128)S(1)}, u32[]{:S(2)}, u32[]{:S(2)}) async-start(s32[3,32,2]{0,2,1:T(2,128)} %bitcast), calls=%async_computation | async-start | bytes 65536 | tf_op jit(solution)/shard_map/all_to_all | solution.py:180
  103.8 0.4 fusion.23
  104.2 0.8 fusion.47
  105.0 0.6 pad_maximum_fusion
  105.6 7.0 %fusion.46 = (bf16[5,8,64,384]{3,2,1,0:T(8,128)(2,1)S(1)}, bf16[5,8,64,384]{3,2,1,0:T(8,128)(2,1)S(1)}, bf16[5,8,64,384]{3,2,1,0:T(8,128)(2,1)S(1)}, bf16[5,8,64...) fusion(bf16[7,10,64,384]{3,2,1,0:T(8,128)(2,1)S(1)} %pad_maximu, ...), kind=kLoop, calls=%fused_computation.149 | loop fusion | bytes 35389440 | tf_op jit(solution)/shard_map/slice | solution.py:41
  112.6 2.4 %fusion.52 = f32[2560,128]{1,0:T(8,128)S(1)} fusion(bf16[2560,384]{1,0:T(8,128)(2,1)} %bitcast.311, bf16[384,128]{1,0:T(8,128)(2,1)S(1)} %bitcast.317), kind=kOutput, calls=%fused_computation.155 | convolution fusion | flops 251658240 | bytes 3375104 | tf_op jit(solution)/shard_map/dot_general | solution.py:42
  115.0 0.7 convolution_add_fusion.7
  115.7 0.7 convolution_add_fusion.6
  116.4 0.7 convolution_add_fusion.5
  117.1 0.7 convolution_add_fusion.4
  117.8 0.7 convolution_add_fusion.3
  118.5 0.7 convolution_add_fusion.2
  119.2 0.7 convolution_add_fusion.1
  119.9 0.7 convolution_add_fusion
  120.8 2.1 %collective-permute-start.2 = (bf16[5,1,64,128]{3,2,1,0:T(8,128)(2,1)S(1)}, bf16[5,1,64,128]{3,2,1,0:T(8,128)(2,1)S(1)}, u32[]{:S(2)}, u32[]{:S(2)}) collective-permute-start(bf16[5,1,64,128]{3,2,1,0:T(8,128)(2,1)S(1)} %slice.194), channel_id=1, source_target_pairs={{1,0},{2,1},{3,2},{4,3},{5,4},{6,5},{7,6},{8,7},{9,8},{10,9},{11,1... | collective-permute-start | bytes 245768 | tf_op jit(solution)/shard_map/ppermute | solution.py:30
  123.0 4.4 %collective-permute-done.2 = bf16[5,1,64,128]{3,2,1,0:T(8,128)(2,1)S(1)} collective-permute-done((bf16[5,1,64,128]{3,2,1,0:T(8,128)(2,1)S(1)}, bf16[5,1,64,128]{3,2,1,0:T(8,128)(2,1)S(1)}, u32[]{:S(2)}, u32[]{:S(2)}) %collective-permute-start.2) | collective-permute-done | bytes 81952 | tf_op jit(solution)/shard_map/ppermute | solution.py:30
  129.7 0.3 fusion.53
  130.2 0.3 convolution_add_fusion.9
  130.5 0.3 convolution_add_fusion.8
  130.9 0.5 copy-done.5
  131.7 0.3 fusion.30
  132.7 0.6 constant_dynamic-update-slice_fusion.31
  133.2 0.6 constant_dynamic-update-slice_fusion.30
  133.8 0.6 constant_dynamic-update-slice_fusion.29
  134.4 0.6 constant_dynamic-update-slice_fusion.28
  134.9 0.6 constant_dynamic-update-slice_fusion.27
  135.5 0.6 constant_dynamic-update-slice_fusion.26
  136.1 0.6 constant_dynamic-update-slice_fusion.25
  136.6 0.6 constant_dynamic-update-slice_fusion.24
  137.2 0.6 constant_dynamic-update-slice_fusion.23
  137.8 0.6 constant_dynamic-update-slice_fusion.22
  138.3 0.6 constant_dynamic-update-slice_fusion.21
  138.9 0.6 constant_dynamic-update-slice_fusion.20
  139.4 0.6 constant_dynamic-update-slice_fusion.19
  140.0 0.6 constant_dynamic-update-slice_fusion.18
  140.6 0.6 constant_dynamic-update-slice_fusion.17
  141.1 0.6 constant_dynamic-update-slice_fusion.16
  141.7 0.6 constant_dynamic-update-slice_fusion.15
  142.3 0.6 constant_dynamic-update-slice_fusion.14
  142.8 0.6 constant_dynamic-update-slice_fusion.13
  143.4 0.6 constant_dynamic-update-slice_fusion.12
  144.0 0.6 constant_dynamic-update-slice_fusion.11
  144.5 0.6 constant_dynamic-update-slice_fusion.10
  145.1 0.6 constant_dynamic-update-slice_fusion.9
  145.7 0.6 constant_dynamic-update-slice_fusion.8
  146.2 0.6 constant_dynamic-update-slice_fusion.7
  146.8 0.6 constant_dynamic-update-slice_fusion.6
  147.4 0.6 constant_dynamic-update-slice_fusion.5
  147.9 0.6 constant_dynamic-update-slice_fusion.4
  148.5 0.6 constant_dynamic-update-slice_fusion.3
  149.1 0.6 constant_dynamic-update-slice_fusion.2
  149.6 0.6 constant_dynamic-update-slice_fusion.1
  150.2 0.6 constant_dynamic-update-slice_fusion
  150.8 12.0 %all-to-all-start.1 = ((bf16[32,3,1,2,128]{4,3,1,2,0:T(2,128)(2,1)}), bf16[32,3,1,2,128]{4,3,1,2,0:T(2,128)(2,1)S(1)}, u32[]{:S(2)}, u32[]{:S(2)}) async-start(bf16[32,3,1,2,128]{4,3,1,2,0:T(2,128)(2,1)} %constant_dynamic-update-slice_fusion), calls=%async_computation.1 | async-start | bytes 98304 | tf_op jit(solution)/shard_map/all_to_all | solution.py:175
  162.9 13.6 %all-to-all-done.1 = bf16[32,3,1,2,128]{4,3,1,2,0:T(2,128)(2,1)S(1)} async-done(((bf16[32,3,1,2,128]{4,3,1,2,0:T(2,128)(2,1)}), bf16[32,3,1,2,128]{4,3,1,2,0:T(2,128)(2,1)S(1)}, u32[]{:S(2)}, u32[]{:S(2)}) %all-to-all-start.1) | async-done | bytes 49184 | tf_op jit(solution)/shard_map/all_to_all | solution.py:175
  176.6 0.8 convolution_convert_fusion
  (79 shorter events, 5.3 us)
Async XLA Ops:
  0.0 131.7 %copy-start = (bf16[128,32]{0,1:T(8,128)(2,1)S(1)}, bf16[128,32]{0,1:T(8,128)(2,1)}, u32[]{:S(2)}) copy-start(bf16[128,32]{0,1:T(8,128)(2,1)} %param.22) | copy-start | bytes 24580
  0.0 80.6 %copy-start.1 = (bf16[1,5,8,64,128]{4,3,2,1,0:T(8,128)(2,1)S(1)}, bf16[1,5,8,64,128]{4,3,2,1,0:T(8,128)(2,1)}, u32[]{:S(2)}) copy-start(bf16[1,5,8,64,128]{4,3,2,1,0:T(8,128)(2,1)} %param.13) | copy-start | bytes 1966084
  0.0 80.6 %copy-start.9 = (f32[128]{0:T(128)S(1)}, f32[128]{0:T(128)}, u32[]{:S(2)}) copy-start(f32[128]{0:T(128)} %param.14) | copy-start | bytes 1540
  0.0 80.6 %copy-start.8 = (f32[128]{0:T(128)S(1)}, f32[128]{0:T(128)}, u32[]{:S(2)}) copy-start(f32[128]{0:T(128)} %param.15) | copy-start | bytes 1540
  1.5 85.5 %copy-start.6 = (s32[1,3,32]{2,0,1:T(1,128)S(1)}, s32[1,3,32]{2,0,1:T(1,128)}, u32[]{:S(2)}) copy-start(s32[1,3,32]{2,0,1:T(1,128)} %param.24) | copy-start | bytes 1156
  43.0 44.4 %copy-start.7 = (s32[1,3,32]{2,0,1:T(1,128)S(1)}, s32[1,3,32]{2,0,1:T(1,128)}, u32[]{:S(2)}) copy-start(s32[1,3,32]{2,0,1:T(1,128)} %param.25) | copy-start | bytes 1156
  43.2 60.5 %copy-start.3 = (bf16[3,3,3,128,128]{4,3,2,1,0:T(8,128)(2,1)S(1)}, bf16[3,3,3,128,128]{4,3,2,1,0:T(8,128)(2,1)}, u32[]{:S(2)}) copy-start(bf16[3,3,3,128,128]{4,3,2,1,0:T(8,128)(2,1)} %param.16) | copy-start | bytes 2654212
  81.2 22.6 %collective-permute-start = (bf16[5,1,64,128]{3,2,1,0:T(8,128)(2,1)S(1)}, bf16[5,1,64,128]{3,2,1,0:T(8,128)(2,1)S(1)}, u32[]{:S(2)}, u32[]{:S(2)}) collective-permute-start(bf16[5,1,64,128]{3,2,1,0:T(8,128)(2,1)S(1)} %get-tuple-element.29), channel_id=1, source_target_pairs={{0,1},{1,2},{2,3},{3,4},{4,5},{5,6},{6,7},{7,8},{8,9},{9,10},{10,1... | collective-permute-start | bytes 245768 | tf_op jit(solution)/shard_map/ppermute | solution.py:18
  83.1 20.7 %collective-permute-start.1 = (bf16[5,1,64,128]{3,2,1,0:T(8,128)(2,1)S(1)}, bf16[5,1,64,128]{3,2,1,0:T(8,128)(2,1)S(1)}, u32[]{:S(2)}, u32[]{:S(2)}) collective-permute-start(bf16[5,1,64,128]{3,2,1,0:T(8,128)(2,1)S(1)} %get-tuple-element.30), channel_id=1, source_target_pairs={{1,0},{2,1},{3,2},{4,3},{5,4},{6,5},{7,6},{8,7},{9,8},{10,9},{11,1... | collective-permute-start | bytes 245768 | tf_op jit(solution)/shard_map/ppermute | solution.py:20
  88.4 62.4 %all-to-all-start = ((s32[3,32,2]{0,2,1:T(2,128)}), s32[3,32,2]{0,2,1:T(2,128)S(1)}, u32[]{:S(2)}, u32[]{:S(2)}) async-start(s32[3,32,2]{0,2,1:T(2,128)} %bitcast), calls=%async_computation | async-start | bytes 65536 | tf_op jit(solution)/shard_map/all_to_all | solution.py:180
  112.6 2.4 %copy-start.2 = (bf16[5,8,64,384]{3,2,1,0:T(8,128)(2,1)S(1)}, bf16[5,8,64,384]{3,2,1,0:T(8,128)(2,1)}, u32[]{:S(2)}) copy-start(bf16[5,8,64,384]{3,2,1,0:T(8,128)(2,1)} %get-tuple-element.12) | copy-start | bytes 5898244
  119.9 0.7 copy-start.13
  120.6 2.4 %copy-start.4 = (bf16[3,3,128,128]{3,2,1,0:T(8,128)(2,1)S(1)}, bf16[3,3,128,128]{3,2,1,0:T(8,128)(2,1)}, u32[]{:S(2)}) copy-start(bf16[3,3,128,128]{3,2,1,0:T(8,128)(2,1)} %param.18) | copy-start | bytes 884740
  120.8 6.5 %collective-permute-start.2 = (bf16[5,1,64,128]{3,2,1,0:T(8,128)(2,1)S(1)}, bf16[5,1,64,128]{3,2,1,0:T(8,128)(2,1)S(1)}, u32[]{:S(2)}, u32[]{:S(2)}) collective-permute-start(bf16[5,1,64,128]{3,2,1,0:T(8,128)(2,1)S(1)} %slice.194), channel_id=1, source_target_pairs={{1,0},{2,1},{3,2},{4,3},{5,4},{6,5},{7,6},{8,7},{9,8},{10,9},{11,1... | collective-permute-start | bytes 245768 | tf_op jit(solution)/shard_map/ppermute | solution.py:30
  130.2 0.7 copy-start.10
  130.5 0.9 copy-start.5
  130.5 1.2 copy-start.11
  130.5 1.2 copy-start.12
  150.8 25.8 %all-to-all-start.1 = ((bf16[32,3,1,2,128]{4,3,1,2,0:T(2,128)(2,1)}), bf16[32,3,1,2,128]{4,3,1,2,0:T(2,128)(2,1)S(1)}, u32[]{:S(2)}, u32[]{:S(2)}) async-start(bf16[32,3,1,2,128]{4,3,1,2,0:T(2,128)(2,1)} %constant_dynamic-update-slice_fusion), calls=%async_computation.1 | async-start | bytes 98304 | tf_op jit(solution)/shard_map/all_to_all | solution.py:175
